TPU v7x, 256 devices: a whole 4x4x8 slice. The times are simulated.
256 devices in a mesh: dp: 16 (over y, x), row: 2 (over core), col: 8 (over z).
Axes of the slice: x: 4, y: 4, z: 8, core: 2. Of those that a mesh axis runs over, the one named last changes fastest.
Arguments:
- grads: bfloat16 [16, 3072, 8192], P('dp', 'row', 'col'), may hold values from -6 to 6
- errors: bfloat16 [16, 3072, 8192], P('dp', 'row', 'col'), may hold values from -4 to 4
- q_init: float32 [8192, 64], P('col'), may hold values from -6 to 6
Outputs:
- new_errors: bfloat16 [16, 3072, 8192], P('dp', 'row', 'col')
- q_factor: float32 [8192, 64], P('col')
All inputs are finite; a program needn't handle non-finite values.
Results may differ from a plain program's by a relative error of at most 0.009.
Values may be sent and summed in bfloat16 or wider, within the bound.
A program may use at most 128 MiB of HBM per device.

v0:
```python
import jax
import jax.numpy as jnp
from jax import lax
from jax.sharding import PartitionSpec as P

ITERS = 7


def orthonormal(left, gram):
    lower = jnp.linalg.cholesky(gram)
    return lax.linalg.triangular_solve(lower, left, left_side=False, lower=True, transpose_a=True)


def shards(grads, errors, q_init):
    merged = (grads[0].astype(jnp.float32) + errors[0].astype(jnp.float32)).astype(jnp.bfloat16)
    replicas = lax.axis_size("dp")
    q_now = q_init
    p_low = None
    for step in range(ITERS):
        q_low = q_now.astype(jnp.bfloat16)
        partial_left = jnp.dot(merged, q_low, preferred_element_type=jnp.float32)
        total = lax.psum(partial_left, ("dp", "col")) / replicas
        gram = lax.psum(jnp.dot(total.T, total, precision=lax.Precision.HIGHEST), "row")
        p_low = orthonormal(total, gram).astype(jnp.bfloat16)
        partial_right = lax.dot_general(
            merged, p_low, (((0,), (0,)), ((), ())), preferred_element_type=jnp.float32
        )
        q_now = lax.psum(partial_right, ("dp", "row")) / replicas
    approx = jnp.dot(p_low, q_now.astype(jnp.bfloat16).T, preferred_element_type=jnp.float32)
    new_errors = (merged.astype(jnp.float32) - approx).astype(jnp.bfloat16)
    return (new_errors[None], q_now)


def solution(mesh):
    return jax.shard_map(
        shards,
        mesh=mesh,
        in_specs=(P("dp", "row", "col"), P("dp", "row", "col"), P("col", None)),
        out_specs=(P("dp", "row", "col"), P("col", None)),
        check_vma=False,
    )
```

profile of v0, /device:TPU:1, one launch (start us, length us, event | category | flops | bytes accessed | tf_op | source)
XLA Modules:
  0.0 2468.0 jit_solution(17352700967499710845)
XLA Ops:
  7.2 4.4 fusion.1
  11.6 1.8 fusion.57
  13.5 214.3 %all-reduce.15.cloned.1.call-done = f32[1536,64]{0,1:T(8,128)} async-done(((f32[1536,64]{0,1:T(8,128)}), f32[1536,64]{0,1:T(8,128)}) %all-reduce.15.cloned.1.call-update) | async-done | bytes 393232 | tf_op jit(solution)/shard_map/psum | solution.py:22
  227.9 1.6 fusion.28
  229.5 8.4 psum.148
  238.0 5.8 cholesky.119
  245.1 4.9 custom-call.11
  253.0 108.4 %all-reduce.17.cloned.1.call-done = f32[1024,64]{0,1:T(8,128)} async-done(((f32[1024,64]{0,1:T(8,128)}), f32[1024,64]{0,1:T(8,128)}) %all-reduce.17.cloned.1.call-update) | async-done | bytes 262160 | tf_op jit(solution)/shard_map/psum | solution.py:28
  361.5 2.8 fusion.44
  364.3 213.0 %all-reduce.19.cloned.1.call-done = f32[1536,64]{0,1:T(8,128)} async-done(((f32[1536,64]{0,1:T(8,128)}), f32[1536,64]{0,1:T(8,128)}) %all-reduce.19.cloned.1.call-update) | async-done | bytes 393232 | tf_op jit(solution)/shard_map/psum | solution.py:22
  577.3 1.6 fusion.25
  578.9 8.4 psum.151
  587.3 5.8 cholesky.130
  594.5 4.9 custom-call.12
  602.4 108.4 %all-reduce.21.cloned.1.call-done = f32[1024,64]{0,1:T(8,128)} async-done(((f32[1024,64]{0,1:T(8,128)}), f32[1024,64]{0,1:T(8,128)}) %all-reduce.21.cloned.1.call-update) | async-done | bytes 262160 | tf_op jit(solution)/shard_map/psum | solution.py:28
  710.8 2.8 fusion.45
  713.7 212.8 %all-reduce.23.cloned.1.call-done = f32[1536,64]{0,1:T(8,128)} async-done(((f32[1536,64]{0,1:T(8,128)}), f32[1536,64]{0,1:T(8,128)}) %all-reduce.23.cloned.1.call-update) | async-done | bytes 393232 | tf_op jit(solution)/shard_map/psum | solution.py:22
  926.5 1.6 fusion.22
  928.1 8.6 psum.154
  936.8 5.8 cholesky.141
  944.0 4.9 custom-call.13
  951.8 108.4 %all-reduce.25.cloned.1.call-done = f32[1024,64]{0,1:T(8,128)} async-done(((f32[1024,64]{0,1:T(8,128)}), f32[1024,64]{0,1:T(8,128)}) %all-reduce.25.cloned.1.call-update) | async-done | bytes 262160 | tf_op jit(solution)/shard_map/psum | solution.py:28
  1060.3 2.8 fusion.46
  1063.1 213.0 %all-reduce.27.cloned.1.call-done = f32[1536,64]{0,1:T(8,128)} async-done(((f32[1536,64]{0,1:T(8,128)}), f32[1536,64]{0,1:T(8,128)}) %all-reduce.27.cloned.1.call-update) | async-done | bytes 393232 | tf_op jit(solution)/shard_map/psum | solution.py:22
  1277.7 8.4 psum.157
  1286.1 5.8 cholesky.152
  1293.3 4.9 custom-call.14
  1301.2 108.4 %all-reduce.29.cloned.1.call-done = f32[1024,64]{0,1:T(8,128)} async-done(((f32[1024,64]{0,1:T(8,128)}), f32[1024,64]{0,1:T(8,128)}) %all-reduce.29.cloned.1.call-update) | async-done | bytes 262160 | tf_op jit(solution)/shard_map/psum | solution.py:28
  1409.6 2.8 fusion.47
  1412.5 213.0 %all-reduce.31.cloned.1.call-done = f32[1536,64]{0,1:T(8,128)} async-done(((f32[1536,64]{0,1:T(8,128)}), f32[1536,64]{0,1:T(8,128)}) %all-reduce.31.cloned.1.call-update) | async-done | bytes 393232 | tf_op jit(solution)/shard_map/psum | solution.py:22
  1627.0 8.4 psum.160
  1635.5 5.8 cholesky.163
  1642.7 4.9 custom-call.15
  1650.6 108.4 %all-reduce.33.cloned.1.call-done = f32[1024,64]{0,1:T(8,128)} async-done(((f32[1024,64]{0,1:T(8,128)}), f32[1024,64]{0,1:T(8,128)}) %all-reduce.33.cloned.1.call-update) | async-done | bytes 262160 | tf_op jit(solution)/shard_map/psum | solution.py:28
  1759.0 2.8 fusion.48
  1762.1 212.7 %all-reduce.35.cloned.1.call-done = f32[1536,64]{0,1:T(8,128)} async-done(((f32[1536,64]{0,1:T(8,128)}), f32[1536,64]{0,1:T(8,128)}) %all-reduce.35.cloned.1.call-update) | async-done | bytes 393232 | tf_op jit(solution)/shard_map/psum | solution.py:22
  1976.4 8.4 psum.163
  1984.9 5.8 cholesky.174
  1992.1 4.9 custom-call.16
  2000.0 108.4 %all-reduce.37.cloned.1.call-done = f32[1024,64]{0,1:T(8,128)} async-done(((f32[1024,64]{0,1:T(8,128)}), f32[1024,64]{0,1:T(8,128)}) %all-reduce.37.cloned.1.call-update) | async-done | bytes 262160 | tf_op jit(solution)/shard_map/psum | solution.py:28
  2108.4 2.8 fusion.49
  2111.2 213.0 %all-reduce.39.cloned.1.call-done = f32[1536,64]{0,1:T(8,128)} async-done(((f32[1536,64]{0,1:T(8,128)}), f32[1536,64]{0,1:T(8,128)}) %all-reduce.39.cloned.1.call-update) | async-done | bytes 393232 | tf_op jit(solution)/shard_map/psum | solution.py:22
  2324.2 1.6 fusion.10
  2325.8 8.4 psum.166
  2334.3 5.8 cholesky.185
  2341.5 4.9 custom-call.17
  2349.3 108.5 %all-reduce.41.cloned.1.call-done = f32[1024,64]{0,1:T(8,128)} async-done(((f32[1024,64]{0,1:T(8,128)}), f32[1024,64]{0,1:T(8,128)}) %all-reduce.41.cloned.1.call-update) | async-done | bytes 262160 | tf_op jit(solution)/shard_map/psum | solution.py:28
  2458.8 2.7 fusion
  (85 shorter events, 37.0 us)
Async XLA Ops:
  7.2 4.5 copy-start.1
  7.2 220.7 %all-reduce.15.cloned.1.call-start = ((), (), s32[]{:S(2)}) async-start(), calls=%async_computation | async-start | bytes 786432 | tf_op jit(solution)/shard_map/psum | solution.py:22
  13.5 348.0 %all-reduce.17.cloned.1.call-start = ((), (), s32[]{:S(2)}) async-start(), calls=%async_computation.1 | async-start | bytes 524288 | tf_op jit(solution)/shard_map/psum | solution.py:28
  253.0 324.3 %all-reduce.19.cloned.1.call-start = ((), (), s32[]{:S(2)}) async-start(), calls=%async_computation.2 | async-start | bytes 786432 | tf_op jit(solution)/shard_map/psum | solution.py:22
  364.2 346.6 %all-reduce.21.cloned.1.call-start = ((), (), s32[]{:S(2)}) async-start(), calls=%async_computation.3 | async-start | bytes 524288 | tf_op jit(solution)/shard_map/psum | solution.py:28
  602.4 324.1 %all-reduce.23.cloned.1.call-start = ((), (), s32[]{:S(2)}) async-start(), calls=%async_computation.4 | async-start | bytes 786432 | tf_op jit(solution)/shard_map/psum | solution.py:22
  713.6 346.6 %all-reduce.25.cloned.1.call-start = ((), (), s32[]{:S(2)}) async-start(), calls=%async_computation.5 | async-start | bytes 524288 | tf_op jit(solution)/shard_map/psum | solution.py:28
  951.8 324.3 %all-reduce.27.cloned.1.call-start = ((), (), s32[]{:S(2)}) async-start(), calls=%async_computation.6 | async-start | bytes 786432 | tf_op jit(solution)/shard_map/psum | solution.py:22
  1063.1 346.6 %all-reduce.29.cloned.1.call-start = ((), (), s32[]{:S(2)}) async-start(), calls=%async_computation.7 | async-start | bytes 524288 | tf_op jit(solution)/shard_map/psum | solution.py:28
  1301.2 324.3 %all-reduce.31.cloned.1.call-start = ((), (), s32[]{:S(2)}) async-start(), calls=%async_computation.8 | async-start | bytes 786432 | tf_op jit(solution)/shard_map/psum | solution.py:22
  1412.4 346.6 %all-reduce.33.cloned.1.call-start = ((), (), s32[]{:S(2)}) async-start(), calls=%async_computation.9 | async-start | bytes 524288 | tf_op jit(solution)/shard_map/psum | solution.py:28
  1650.5 324.3 %all-reduce.35.cloned.1.call-start = ((), (), s32[]{:S(2)}) async-start(), calls=%async_computation.10 | async-start | bytes 786432 | tf_op jit(solution)/shard_map/psum | solution.py:22
  1761.8 346.6 %all-reduce.37.cloned.1.call-start = ((), (), s32[]{:S(2)}) async-start(), calls=%async_computation.11 | async-start | bytes 524288 | tf_op jit(solution)/shard_map/psum | solution.py:28
  1999.9 324.3 %all-reduce.39.cloned.1.call-start = ((), (), s32[]{:S(2)}) async-start(), calls=%async_computation.12 | async-start | bytes 786432 | tf_op jit(solution)/shard_map/psum | solution.py:22
  2111.2 346.6 %all-reduce.41.cloned.1.call-start = ((), (), s32[]{:S(2)}) async-start(), calls=%async_computation.13 | async-start | bytes 524288 | tf_op jit(solution)/shard_map/psum | solution.py:28
  2458.8 2.7 copy-start
Sparse Core Ops, SparseCore 0:
  14.0 213.8 all-reduce.14
  253.1 108.3 all-reduce.16
  367.5 209.7 all-reduce.18
  602.5 108.3 all-reduce.20
  716.7 209.7 all-reduce.22
  951.9 108.3 all-reduce.24
  1066.2 209.7 all-reduce.26
  1301.3 108.3 all-reduce.28
  1415.6 209.7 all-reduce.30
  1650.7 108.3 all-reduce.32
  1765.0 209.7 all-reduce.34
  2000.1 108.2 all-reduce.36
  2114.4 209.7 all-reduce.38
  2349.4 108.3 all-reduce.40
where the time goes:
time: 2470 us
  waiting for transfers between devices  2250 us (91%)
  other arithmetic  89.9 us (4%)
  blocking collectives  58.9 us (2%)
  matrix products  52.6 us (2%)
    psum x7, waiting for transfers between devices, shards(): total = lax.psum(partial_left, ('dp', 'col')) / replicas  1490 us
    psum x7, waiting for transfers between devices, shards(): q_now = lax.psum(partial_right, ('dp', 'row')) / replicas  759 us
    psum x7, blocking collectives, shards(): lax.psum(jnp.dot(total.T, total, precision=lax.Precision.HIGHEST), 'row')  58.9 us
  transfers between devices with their start and end apart: 14, of which 14 were waited for; matrix products, arithmetic and copies ran while one was open for 0% of the time, Pallas kernels for 0%

commit v1 on v0

v1 whole, which is shorter than its diff:
```python
import functools

import jax
import jax.numpy as jnp
from jax import lax
from jax.experimental import pallas as pl
from jax.experimental.pallas import tpu as pltpu
from jax.sharding import PartitionSpec as P

MESH = pl.DeviceIdType.MESH
ITERS = 7
F32, BF16 = jnp.float32, jnp.bfloat16
NT = (((1,), (1,)), ((), ()))
TN = (((0,), (0,)), ((), ()))
SIDE = 4


def lanes(shape):
    return lax.broadcasted_iota(jnp.int32, shape, 1)


def halves(x):
    high = x.astype(BF16)
    low = (x - high.astype(F32)).astype(BF16)
    return jnp.where(lanes(x.shape) < 64, high, low)


def fold(x):
    return x + pltpu.roll(x, 64, 1)


def inverse_factor(gram):
    shape = (64, 128)
    lane, row = lanes(shape), lax.broadcasted_iota(jnp.int32, shape, 0)
    w = jnp.where(lane < 64, gram, (lane - 64 == row).astype(F32))
    for j in range(64):
        g = 8 * (j // 8)
        tail = w[g:]
        scale = tail[:, j : j + 1] * (1.0 / w[j : j + 1, j : j + 1])
        scale = jnp.where(row[g:, :1] > j, scale, 0.0)
        tail = tail - scale * w[j : j + 1]
        w = jnp.concatenate([w[:g], tail], 0) if g else tail
    pivot = jnp.sum(jnp.where(lane == row, w, 0.0), axis=1, keepdims=True)
    w = jnp.where(lane < 64, 0.0, w * lax.rsqrt(pivot))
    w = fold(w)
    high = w.astype(BF16)
    low = (w - high.astype(F32)).astype(BF16)
    both = jnp.concatenate([high, low], 1)
    return jnp.concatenate([both, both], 0)


def kernel(
    replicas, planes, g_ref, e_ref, q_ref, err_ref, qf_ref,
    g_buf, e_buf, merged, rs_buf, mz, own, kpart, kfull, zbuf, zp, zp_own, v, pp, factor, ysend, yrecv, gsend, grecv,
    qsend, qrecv, qlow, plow, out_buf,
    g_sem, e_sem, rs_s, rs_r, ag_s, ag_r, own_sem, z1_s, z1_r, z2_s, z2_r, z3_s, z3_r, it_s, it_r, y_sem, gr_sem, q_sem, o_sem,
):
    dp, core, z = lax.axis_index("dp"), lax.axis_index("row"), lax.axis_index("col")
    y, x = dp // SIDE, dp % SIDE
    rows, cols = merged.shape
    part = rows // replicas
    half = kfull.shape[1] // 2
    quarter = kfull.shape[0] // 4

    def peer(i):
        return ((y + i // SIDE) % SIDE) * SIDE + (x + i % SIDE) % SIDE

    def source(i):
        return ((y + SIDE - i // SIDE) % SIDE) * SIDE + (x + SIDE - i % SIDE) % SIDE

    def at(i):
        return pl.ds(pl.multiple_of(i * part, part), part)

    def zpeer(i):
        return (z + i) % planes

    def zsource(i):
        return (z + planes - i) % planes

    def remote(src, dst, ssem, rsem, **device):
        return pltpu.make_async_remote_copy(
            src_ref=src, dst_ref=dst, send_sem=ssem, recv_sem=rsem, device_id=device, device_id_type=MESH
        )

    def each(lo, hi, body):
        def step(i, carry):
            body(i)
            return carry

        lax.fori_loop(lo, hi, step, 0)

    def load(i):
        here = at(peer(i))
        pltpu.make_async_copy(g_ref.at[0, here], g_buf.at[here], g_sem.at[i]).start()
        pltpu.make_async_copy(e_ref.at[0, here], e_buf.at[here], e_sem.at[i]).start()

    each(0, replicas, load)
    barrier = pltpu.get_barrier_semaphore()
    each(1, replicas, lambda i: pl.semaphore_signal(barrier, inc=1, device_id={"dp": peer(i)}, device_id_type=MESH))
    each(1, planes, lambda i: pl.semaphore_signal(barrier, inc=1, device_id={"col": zpeer(i)}, device_id_type=MESH))
    pl.semaphore_signal(barrier, inc=1, device_id={"row": 1 - core}, device_id_type=MESH)
    pl.semaphore_wait(barrier, replicas - 1 + planes - 1 + 1)

    def scatter(i):
        return remote(merged.at[at(peer(i))], rs_buf.at[i], rs_s.at[i], rs_r.at[i], dp=peer(i))

    def merge(i):
        here = at(peer(i))
        pltpu.make_async_copy(g_ref.at[0, here], g_buf.at[here], g_sem.at[i]).wait()
        pltpu.make_async_copy(e_ref.at[0, here], e_buf.at[here], e_sem.at[i]).wait()
        merged[here, :] = (g_buf[here, :].astype(F32) + e_buf[here, :].astype(F32)).astype(BF16)

    def merge_send(i):
        merge(i)
        scatter(i).start()

    each(1, replicas, merge_send)
    merge(0)
    each(1, replicas, lambda i: scatter(i).wait_recv())

    def mean(i):
        sub = pl.ds(pl.multiple_of(i * 16, 16), 16)
        total = merged[pl.ds(pl.multiple_of(dp * part + i * 16, 16), 16), :].astype(F32)
        for r in range(1, replicas):
            total = total + rs_buf[r, sub, :].astype(F32)
        low = (total * (1.0 / replicas)).astype(BF16)
        mz[pl.ds(pl.multiple_of(dp * part + i * 16, 16), 16), :] = low
        own[core, sub, :] = low

    each(0, part // 16, mean)

    def gather(i, owner):
        return remote(mz.at[at(owner)], mz.at[at(owner)], ag_s.at[i], ag_r.at[i], dp=peer(i))

    swap_own = remote(own.at[core], own.at[core], own_sem.at[0], own_sem.at[1], row=1 - core)
    each(1, replicas, lambda i: gather(i, dp).start())
    swap_own.start()

    first = jnp.dot(own[core], q_ref[...].astype(BF16), preferred_element_type=F32)
    zp_own[...] = halves(jnp.concatenate([first, first], 1))

    def first_sum(i):
        return remote(zp_own, zp.at[i], z1_s.at[i], z1_r.at[i], col=zpeer(i))

    each(1, planes, lambda i: first_sum(i).start())
    each(1, planes, lambda i: first_sum(i).wait_recv())
    zp[0] = zp_own[...]
    total = zp[z].astype(F32)
    for r in range(1, planes):
        total = total + zp[(z + planes - r) % planes].astype(F32)
    v[0, at(dp), :] = halves(fold(total))

    def spread(slot, i, owner):
        return remote(v.at[slot, at(owner)], v.at[slot, at(owner)], it_s.at[slot, i], it_r.at[slot, i], dp=peer(i))

    each(1, replicas, lambda i: spread(0, i, dp).start())

    each(1, replicas, lambda i: gather(i, source(i)).wait_recv())
    remote(own.at[1 - core], own.at[1 - core], own_sem.at[0], own_sem.at[1], row=1 - core).wait_recv()
    tile = 256

    def plane_term(i):
        here = pl.ds(pl.multiple_of(i * tile, tile), tile)
        for c in range(2):
            term = lax.dot_general(own[c], mz[here, :], NT, preferred_element_type=F32)
            kpart[c * part : (c + 1) * part, here] = term.astype(BF16)

    each(0, rows // tile, plane_term)

    def piece(ref, i):
        return ref.at[
            pl.ds(pl.multiple_of(i // 2 * quarter, quarter), quarter),
            pl.ds(pl.multiple_of(i % 2 * half, half), half),
        ]

    def k_scatter(i):
        return remote(piece(kpart, zpeer(i)), zbuf.at[i], z2_s.at[i], z2_r.at[i], col=zpeer(i))

    def k_gather(i, owner):
        return remote(piece(kfull, owner), piece(kfull, owner), z3_s.at[i], z3_r.at[i], col=zpeer(i))

    each(1, planes, lambda i: k_scatter(i).start())
    each(1, planes, lambda i: k_scatter(i).wait_recv())
    mine_rows, mine_cols = z // 2 * quarter, pl.ds(pl.multiple_of(z % 2 * half, half), half)

    def k_sum(i):
        here = pl.ds(pl.multiple_of(mine_rows + i * 16, 16), 16)
        total = kpart[here, mine_cols].astype(F32)
        for r in range(1, planes):
            total = total + zbuf[r, pl.ds(pl.multiple_of(i * 16, 16), 16), :].astype(F32)
        kfull[here, mine_cols] = total.astype(BF16)

    each(0, quarter // 16, k_sum)
    each(1, planes, lambda i: k_gather(i, z).start())
    each(1, planes, lambda i: k_gather(i, zsource(i)).wait_recv())

    eye = (lax.broadcasted_iota(jnp.int32, (128, 256), 0) % 64 == lanes((128, 256)) % 64) & (lanes((128, 256)) < 128)
    factor[...] = eye.astype(F32).astype(BF16)

    def apply(value):
        twice = jnp.concatenate([value, value], 1)
        return lax.dot_general(twice, factor[...], NT, preferred_element_type=F32)

    def swap_y(slot):
        return remote(ysend.at[slot], yrecv.at[slot], y_sem.at[0, slot], y_sem.at[1, slot], row=1 - core)

    def swap_gram(slot):
        return remote(gsend.at[slot], grecv.at[slot], gr_sem.at[0, slot], gr_sem.at[1, slot], row=1 - core)

    def iterate(k):
        slot, after = k % 2, (k + 1) % 2
        each(1, replicas, lambda i: spread(slot, i, source(i)).wait_recv())
        pp[...] = halves(apply(v[slot]))

        @pl.when(k < ITERS - 1)
        def _():
            theirs = pl.ds(pl.multiple_of((1 - core) * part, part), part)
            ysend[slot] = jnp.dot(kfull[theirs, :], pp[...], preferred_element_type=F32)
            swap_y(slot).start()

        gsend[slot] = lax.dot_general(pp[...], pp[...], TN, preferred_element_type=F32)
        swap_gram(slot).start()

        @pl.when(k < ITERS - 1)
        def _():
            ours = pl.ds(pl.multiple_of(core * part, part), part)
            term = jnp.dot(kfull[ours, :], pp[...], preferred_element_type=F32)
            swap_y(slot).wait_recv()
            v[after, at(dp), :] = halves(fold(term + yrecv[slot]))
            each(1, replicas, lambda i: spread(after, i, dp).start())

        swap_gram(slot).wait_recv()
        gram = fold(gsend[slot] + grecv[slot])
        factor[...] = inverse_factor(gram[:64] + gram[64:])
        swap_gram(slot).wait_send()
        each(1, replicas, lambda i: spread(slot, i, dp).wait_send())

        @pl.when(k < ITERS - 1)
        def _():
            swap_y(slot).wait_send()

    each(0, ITERS, iterate)

    plow[...] = apply(pp[...])[:, :64].astype(BF16)
    qsend[...] = lax.dot_general(plow[...], mz[...], TN, preferred_element_type=F32)
    swap_q = remote(qsend, qrecv, q_sem.at[0], q_sem.at[1], row=1 - core)
    swap_q.start()
    swap_q.wait_recv()
    q_t = qsend[...] + qrecv[...]
    qlow[...] = q_t.astype(BF16)
    qf_ref[...] = q_t.T

    def left_over(i):
        here = at(i)
        approx = jnp.dot(plow[here, :], qlow[...], preferred_element_type=F32)
        out_buf[here, :] = (merged[here, :].astype(F32) - approx).astype(BF16)
        pltpu.make_async_copy(out_buf.at[here], err_ref.at[0, here], o_sem.at[i]).start()

    each(0, replicas, left_over)

    swap_q.wait_send()
    swap_own.wait_send()
    each(1, replicas, lambda i: scatter(i).wait_send())
    each(1, replicas, lambda i: gather(i, dp).wait_send())
    each(1, planes, lambda i: first_sum(i).wait_send())
    each(1, planes, lambda i: k_scatter(i).wait_send())
    each(1, planes, lambda i: k_gather(i, z).wait_send())

    def stored(i):
        here = at(i)
        pltpu.make_async_copy(out_buf.at[here], err_ref.at[0, here], o_sem.at[i]).wait()

    each(0, replicas, stored)


def solution(mesh):
    replicas, planes = mesh.shape["dp"], mesh.shape["col"]

    def shards(grads, errors, q_init):
        _, rows, cols = grads.shape
        part = rows // replicas
        rank = q_init.shape[1]
        dma = pltpu.SemaphoreType.DMA
        whole = pltpu.VMEM((rows, cols), BF16)
        chip = 2 * part
        scratch = [
            whole, whole, whole,
            pltpu.VMEM((replicas, part, cols), BF16),
            whole,
            pltpu.VMEM((2, part, cols), BF16),
            pltpu.VMEM((chip, rows), BF16),
            pltpu.VMEM((chip, rows), BF16),
            pltpu.VMEM((planes, chip // 4, rows // 2), BF16),
            pltpu.VMEM((planes, part, 128), BF16),
            pltpu.VMEM((part, 128), BF16),
            pltpu.VMEM((2, rows, 128), BF16),
            pltpu.VMEM((rows, 128), BF16),
            pltpu.VMEM((128, 256), BF16),
            pltpu.VMEM((2, part, 128), F32), pltpu.VMEM((2, part, 128), F32),
            pltpu.VMEM((2, 128, 128), F32), pltpu.VMEM((2, 128, 128), F32),
            pltpu.VMEM((rank, cols), F32), pltpu.VMEM((rank, cols), F32),
            pltpu.VMEM((rank, cols), BF16),
            pltpu.VMEM((rows, rank), BF16),
            whole,
            dma((replicas,)), dma((replicas,)),
            dma((replicas,)), dma((replicas,)),
            dma((replicas,)), dma((replicas,)),
            dma((2,)),
            dma((planes,)), dma((planes,)), dma((planes,)), dma((planes,)), dma((planes,)), dma((planes,)),
            dma((2, replicas)), dma((2, replicas)),
            dma((2, 2)), dma((2, 2)), dma((2,)),
            dma((replicas,)),
        ]
        return pl.pallas_call(
            functools.partial(kernel, replicas, planes),
            out_shape=(
                jax.ShapeDtypeStruct(grads.shape, BF16),
                jax.ShapeDtypeStruct(q_init.shape, F32),
            ),
            in_specs=[pl.BlockSpec(memory_space=pl.ANY)] * 2 + [pl.BlockSpec(memory_space=pltpu.VMEM)],
            out_specs=(pl.BlockSpec(memory_space=pl.ANY), pl.BlockSpec(memory_space=pltpu.VMEM)),
            scratch_shapes=scratch,
            compiler_params=pltpu.CompilerParams(
                collective_id=0, has_side_effects=True, vmem_limit_bytes=48 * 2**20
            ),
            name="power_round",
        )(grads, errors, q_init)

    return jax.shard_map(
        shards,
        mesh=mesh,
        in_specs=(P("dp", "row", "col"), P("dp", "row", "col"), P("col", None)),
        out_specs=(P("dp", "row", "col"), P("col", None)),
        check_vma=False,
    )
```

time: 2470 us -> 229 us (0.09)
  waiting for transfers between devices: 2250 us -> 0 us
  Pallas kernels: 0 us -> 221 us
  other arithmetic: 89.9 us -> 0 us
  blocking collectives: 58.9 us -> 0 us
  matrix products: 52.6 us -> 0 us
    psum x14 -> x0, waiting for transfers between devices: 2250 us -> none  [the longest x7 1490 us: shards(): total = lax.psum(partial_left, ('dp', 'col')) / replicas]
    pallas_call x0 -> x1, Pallas kernels: none -> 221 us  [shards(): pl.pallas_call(functools.partial(kernel, replicas, planes), out_shape=(ja...]
    another operation x35 -> x0, other arithmetic: 84.5 us -> none  [the longest x21 45.6 us: orthonormal(): lower = jnp.linalg.cholesky(gram)]
    psum x7 -> x0, blocking collectives: 58.9 us -> none  [shards(): lax.psum(jnp.dot(total.T, total, precision=lax.Precision.HIGHEST), 'row')]
    dot_general x22 -> x0, matrix products: 41.9 us -> none  [the longest x7 18.5 us: shards(): partial_left = jnp.dot(merged, q_low, preferred_element_type=jnp.float32)]
  transfers between devices with their start and end apart: 14 -> 0, of which waited for: 14 -> 0; matrix products, arithmetic and copies ran while one was open for 0% -> 0% of each run, Pallas kernels for 0% -> 0%
where the time goes in v1:
time: 229 us
  Pallas kernels  221 us (97%)
  local copies, waits for them, and re-layouts  7.37 us (3%)
    pallas_call x1, Pallas kernels, shards(): pl.pallas_call(functools.partial(kernel, replicas, planes), out_shape=(ja...  221 us
    unnamed x6, local copies, waits for them, and re-layouts  5.44 us

profile of v1, /device:TPU:1, one launch (start us, length us, event | category | flops | bytes accessed | tf_op | source)
XLA Modules:
  0.0 228.8 jit_solution(16644844539728238692)
XLA Ops:
  0.6 1.9 copy.5.q_ref
  2.6 0.0 copy-start
  2.6 1.0 copy-done
  3.6 220.8 %power_round.1 = (bf16[1,1536,1024]{2,1,0:T(8,128)(2,1)S(1)}, f32[1024,64]{1,0:T(8,128)S(1)}) custom-call(bf16[1,1536,1024]{2,1,0:T(8,128)(2,1)} %g_ref.1, bf16[1,1536,1024]{2,1,0:T(8,128)(2,1)} %e_ref.1, f32[1024,64]{1,0:T(8,128)S(1)} %copy-done), custom_call_target="tpu_custom_call" | custom-call | tf_op jit(solution)/shard_map/power_round/pallas_call | solution.py:314
  224.4 0.0 copy-start.1
  224.5 0.8 copy-done.1
  225.2 1.9 copy.6
  227.2 1.7 copy.8
Async XLA Ops:
  2.6 1.0 copy-start
  224.4 0.8 copy-start.1

commit v2 on v1

v2 whole, which is shorter than its diff:
```python
import functools

import jax
import jax.numpy as jnp
from jax import lax
from jax.experimental import pallas as pl
from jax.experimental.pallas import tpu as pltpu
from jax.sharding import PartitionSpec as P

MESH = pl.DeviceIdType.MESH
ITERS = 7
F32, BF16 = jnp.float32, jnp.bfloat16
NT = (((1,), (1,)), ((), ()))
TN = (((0,), (0,)), ((), ()))
SIDE = 4


def lanes(shape):
    return lax.broadcasted_iota(jnp.int32, shape, 1)


def halves(x):
    high = x.astype(BF16)
    low = (x - high.astype(F32)).astype(BF16)
    return jnp.where(lanes(x.shape) < 64, high, low)


def fold(x):
    return x + pltpu.roll(x, 64, 1)


def inverse_factor(gram):
    shape = (64, 128)
    lane, row = lanes(shape), lax.broadcasted_iota(jnp.int32, shape, 0)
    w = jnp.where(lane < 64, gram, (lane - 64 == row).astype(F32))
    for j in range(64):
        g = 8 * (j // 8)
        tail = w[g:]
        scale = tail[:, j : j + 1] * (1.0 / w[j : j + 1, j : j + 1])
        scale = jnp.where(row[g:, :1] > j, scale, 0.0)
        tail = tail - scale * w[j : j + 1]
        w = jnp.concatenate([w[:g], tail], 0) if g else tail
    pivot = jnp.sum(jnp.where(lane == row, w, 0.0), axis=1, keepdims=True)
    w = jnp.where(lane < 64, 0.0, w * lax.rsqrt(pivot))
    w = fold(w)
    high = w.astype(BF16)
    low = (w - high.astype(F32)).astype(BF16)
    both = jnp.concatenate([high, low], 1)
    return jnp.concatenate([both, both], 0)


def kernel(
    replicas, planes, g_ref, e_ref, q_ref, err_ref, qt_ref,
    g_buf, e_buf, merged, rsa, rsb, sa, sb, rs2a, rs2b, mz, own, kk, zbuf, zp, zown, v, pp, factor, ybuf, yrecv, ytot,
    gsend, grecv, qsend, qrecv, qlow, plow,
    g_sem, e_sem, rs_s, rs_r, ag_s, ag_r, own_sem, z1_s, z1_r, z2_s, z2_r, z3_s, z3_r, it_s, it_r, y_sem, gr_sem, q_sem,
):
    dp, core, z = lax.axis_index("dp"), lax.axis_index("row"), lax.axis_index("col")
    y, x = dp // SIDE, dp % SIDE
    _, _, part, cols = merged.shape
    rows = replicas * part
    first, second = pl.ds(0, cols // 2), pl.ds(cols // 2, cols // 2)
    half, quarter = rows // 2, 2 * part // 4

    def up(a, i):
        return (a + i) % SIDE

    def down(a, i):
        return (a + SIDE - i) % SIDE

    def at(i):
        return pl.ds(pl.multiple_of(i * part, part), part)

    def zpeer(i):
        return (z + i) % planes

    def zsource(i):
        return (z + planes - i) % planes

    def remote(src, dst, ssem, rsem, **device):
        return pltpu.make_async_remote_copy(
            src_ref=src, dst_ref=dst, send_sem=ssem, recv_sem=rsem, device_id=device, device_id_type=MESH
        )

    def each(lo, hi, body):
        def step(i, carry):
            body(i)
            return carry

        lax.fori_loop(lo, hi, step, 0)

    def loads(i):
        yi, xi = i % SIDE, up(x, i // SIDE + 1)
        here = at(yi * SIDE + xi)
        return (
            pltpu.make_async_copy(g_ref.at[0, here], g_buf.at[yi, xi], g_sem.at[i]),
            pltpu.make_async_copy(e_ref.at[0, here], e_buf.at[yi, xi], e_sem.at[i]),
        )

    def load(i):
        for copy in loads(i):
            copy.start()

    def peer(i):
        return up(y, i // SIDE) * SIDE + up(x, i % SIDE)

    def source(i):
        return down(y, i // SIDE) * SIDE + down(x, i % SIDE)

    each(0, replicas, load)
    barrier = pltpu.get_barrier_semaphore()
    each(1, replicas, lambda i: pl.semaphore_signal(barrier, inc=1, device_id={"dp": peer(i)}, device_id_type=MESH))
    each(1, planes, lambda i: pl.semaphore_signal(barrier, inc=1, device_id={"col": zpeer(i)}, device_id_type=MESH))
    pl.semaphore_signal(barrier, inc=1, device_id={"row": 1 - core}, device_id_type=MESH)
    pl.semaphore_wait(barrier, replicas - 1 + planes - 1 + 1)

    def scatter_a(i):
        to = up(x, i)
        return remote(merged.at[:, to, :, first], rsa.at[i], rs_s.at[0, i], rs_r.at[0, i], dp=y * SIDE + to)

    def scatter_b(i):
        to = up(y, i)
        return remote(merged.at[to, :, :, second], rsb.at[i], rs_s.at[1, i], rs_r.at[1, i], dp=to * SIDE + x)

    def merge(i):
        yi, xi = i % SIDE, up(x, i // SIDE + 1)
        for copy in loads(i):
            copy.wait()
        merged[yi, xi] = (g_buf[yi, xi].astype(F32) + e_buf[yi, xi].astype(F32)).astype(BF16)

    def merge_send(i):
        each((i - 1) * SIDE, i * SIDE, merge)
        scatter_a(i).start()

    each(1, SIDE, merge_send)
    each((SIDE - 1) * SIDE, SIDE * SIDE, merge)
    each(1, SIDE, lambda i: scatter_b(i).start())

    def scatter_a2(i):
        return remote(sa.at[i], rs2a.at[i], rs_s.at[2, i], rs_r.at[2, i], dp=up(y, i) * SIDE + x)

    def scatter_b2(i):
        return remote(sb.at[i], rs2b.at[i], rs_s.at[3, i], rs_r.at[3, i], dp=y * SIDE + up(x, i))

    def four_a(to):
        total = merged[to, x, :, first].astype(F32)
        for r in range(1, SIDE):
            total = total + rsa[r, to].astype(F32)
        return total

    def four_b(to):
        total = merged[y, to, :, second].astype(F32)
        for r in range(1, SIDE):
            total = total + rsb[r, to].astype(F32)
        return total

    def send_a(i):
        sa[i] = four_a(up(y, i)).astype(BF16)
        scatter_a2(i).start()

    def send_b(i):
        sb[i] = four_b(up(x, i)).astype(BF16)
        scatter_b2(i).start()

    each(1, SIDE, lambda i: scatter_a(i).wait_recv())
    each(1, SIDE, send_a)
    each(1, SIDE, lambda i: scatter_b(i).wait_recv())
    each(1, SIDE, send_b)

    def mean(total, others, columns):
        for r in range(1, SIDE):
            total = total + others[r].astype(F32)
        low = (total * (1.0 / replicas)).astype(BF16)
        mz[y, x, :, columns] = low
        own[core, :, columns] = low

    def gather_a(i, xi):
        block = mz.at[y, xi, :, first]
        return remote(block, block, ag_s.at[0, i], ag_r.at[0, i], dp=y * SIDE + up(x, i))

    def gather_b(i, yi):
        block = mz.at[yi, x, :, second]
        return remote(block, block, ag_s.at[1, i], ag_r.at[1, i], dp=up(y, i) * SIDE + x)

    def gather_a2(i, yi):
        block = mz.at[yi, :, :, first]
        return remote(block, block, ag_s.at[2, i], ag_r.at[2, i], dp=up(y, i) * SIDE + x)

    def gather_b2(i, xi):
        block = mz.at[:, xi, :, second]
        return remote(block, block, ag_s.at[3, i], ag_r.at[3, i], dp=y * SIDE + up(x, i))

    total = four_a(y)
    each(1, SIDE, lambda i: scatter_a2(i).wait_recv())
    mean(total, rs2a, first)
    each(1, SIDE, lambda i: gather_a(i, x).start())
    total = four_b(x)
    each(1, SIDE, lambda i: scatter_b2(i).wait_recv())
    mean(total, rs2b, second)
    each(1, SIDE, lambda i: gather_b(i, y).start())
    swap_own = remote(own.at[core], own.at[core], own_sem.at[0], own_sem.at[1], row=1 - core)
    swap_own.start()

    def z_copy(which, i):
        return remote(zown.at[which], zp.at[which, i], z1_s.at[which, i], z1_r.at[which, i], col=zpeer(i))

    def z_send(which, term):
        zown[which] = halves(term)
        each(1, planes, lambda i: z_copy(which, i).start())

    def z_total(which):
        each(1, planes, lambda i: z_copy(which, i).wait_recv())
        zp[which, 0] = zown[which]
        total = zp[which, z].astype(F32)
        for r in range(1, planes):
            total = total + zp[which, (z + planes - r) % planes].astype(F32)
        return fold(total)

    def spread(slot, i, owner):
        return remote(v.at[slot, at(owner)], v.at[slot, at(owner)], it_s.at[slot, i], it_r.at[slot, i], dp=peer(i))

    term = lax.dot_general(own[core], q_ref[...].astype(BF16), NT, preferred_element_type=F32)
    z_send(0, jnp.concatenate([term, term], 1))
    each(1, SIDE, lambda i: gather_a(i, down(x, i)).wait_recv())
    each(1, SIDE, lambda i: gather_a2(i, y).start())
    each(1, SIDE, lambda i: gather_b(i, down(y, i)).wait_recv())
    each(1, SIDE, lambda i: gather_b2(i, x).start())
    v[0, at(dp), :] = halves(z_total(0))
    each(1, replicas, lambda i: spread(0, i, dp).start())

    remote(own.at[1 - core], own.at[1 - core], own_sem.at[0], own_sem.at[1], row=1 - core).wait_recv()
    each(1, SIDE, lambda i: gather_a2(i, down(y, i)).wait_recv())
    each(1, SIDE, lambda i: gather_b2(i, down(x, i)).wait_recv())
    tile = SIDE * part

    def plane_term(i):
        block = mz[i].reshape(tile, cols)
        for c in range(2):
            term = lax.dot_general(own[c], block, NT, preferred_element_type=F32)
            kk[0, c * part : (c + 1) * part, pl.ds(pl.multiple_of(i * tile, tile), tile)] = term.astype(BF16)

    each(0, SIDE, plane_term)

    def piece(which, i):
        return kk.at[
            which,
            pl.ds(pl.multiple_of(i // 2 * quarter, quarter), quarter),
            pl.ds(pl.multiple_of(i % 2 * half, half), half),
        ]

    def k_scatter(i):
        return remote(piece(0, zpeer(i)), zbuf.at[i], z2_s.at[i], z2_r.at[i], col=zpeer(i))

    def k_gather(i, owner):
        return remote(piece(1, owner), piece(1, owner), z3_s.at[i], z3_r.at[i], col=zpeer(i))

    def k_sum(i):
        here = pl.ds(pl.multiple_of(z // 2 * quarter + i * 16, 16), 16)
        mine = pl.ds(pl.multiple_of(z % 2 * half, half), half)
        total = kk[0, here, mine].astype(F32)
        for r in range(1, planes):
            total = total + zbuf[r, pl.ds(pl.multiple_of(i * 16, 16), 16), :].astype(F32)
        kk[1, here, mine] = total.astype(BF16)

    each(1, planes, lambda i: k_scatter(i).start())

    eye = (lax.broadcasted_iota(jnp.int32, (128, 256), 0) % 64 == lanes((128, 256)) % 64) & (lanes((128, 256)) < 128)
    factor[...] = eye.astype(F32).astype(BF16)

    def apply(value):
        twice = jnp.concatenate([value, value], 1)
        return lax.dot_general(twice, factor[...], NT, preferred_element_type=F32)

    def swap_y(slot):
        return remote(ybuf.at[1 - core], yrecv.at[slot], y_sem.at[0, slot], y_sem.at[1, slot], row=1 - core)

    def swap_gram(slot):
        return remote(gsend, grecv.at[slot], gr_sem.at[0, slot], gr_sem.at[1, slot], row=1 - core)

    swap_q = remote(qsend, qrecv, q_sem.at[0], q_sem.at[1], row=1 - core)

    def iterate(k):
        slot, after = k % 2, (k + 1) % 2
        each(1, replicas, lambda i: spread(slot, i, source(i)).wait_recv())
        pp[...] = halves(apply(v[slot]))

        @pl.when(k == 1)
        def _():
            each(1, planes, lambda i: k_gather(i, zsource(i)).wait_recv())

        @pl.when(k < ITERS - 1)
        def _():
            which = (k + ITERS - 1) // ITERS
            ybuf[...] = jnp.dot(kk[which], pp[...], preferred_element_type=F32).reshape(ybuf.shape)
            swap_y(slot).start()

        gsend[...] = lax.dot_general(pp[...], pp[...], TN, preferred_element_type=F32)
        swap_gram(slot).start()

        @pl.when(k < ITERS - 1)
        def _():
            swap_y(slot).wait_recv()
            ytot[...] = fold(ybuf[core] + yrecv[slot])

        @pl.when(k == 0)
        def _():
            z_send(1, ytot[...])
            ytot[...] = z_total(1)

        @pl.when(k < ITERS - 1)
        def _():
            v[after, at(dp), :] = halves(ytot[...])
            each(1, replicas, lambda i: spread(after, i, dp).start())

        @pl.when(k == 0)
        def _():
            each(1, planes, lambda i: k_scatter(i).wait_recv())
            each(0, quarter // 16, k_sum)
            each(1, planes, lambda i: k_gather(i, z).start())

        @pl.when(k == ITERS - 1)
        def _():
            both = lax.dot_general(pp[...], mz[...].reshape(rows, cols), TN, preferred_element_type=F32)
            qsend[...] = both[:64] + both[64:]
            swap_q.start()

        swap_gram(slot).wait_recv()
        gram = fold(gsend[...] + grecv[slot])
        factor[...] = inverse_factor(gram[:64] + gram[64:])
        swap_gram(slot).wait_send()
        each(1, replicas, lambda i: spread(slot, i, dp).wait_send())

        @pl.when(k < ITERS - 1)
        def _():
            swap_y(slot).wait_send()

    each(0, ITERS, iterate)

    swap_q.wait_recv()
    q_t = qsend[...] + qrecv[...]
    high = q_t.astype(BF16)
    low = (q_t - high.astype(F32)).astype(BF16)
    q_t = jnp.dot(factor[:64, :], jnp.concatenate([high, low, high, low], 0), preferred_element_type=F32)
    qt_ref[...] = q_t
    qlow[...] = q_t.astype(BF16)
    plow[...] = apply(pp[...])[:, :64].astype(BF16)

    def left_over(i):
        approx = jnp.dot(plow[at(i), :], qlow[...], preferred_element_type=F32)
        err_ref[0, at(i), :] = (merged[i // SIDE, i % SIDE].astype(F32) - approx).astype(BF16)

    each(0, replicas, left_over)

    swap_q.wait_send()
    swap_own.wait_send()

    def sent(i):
        for copy in (scatter_a(i), scatter_b(i), scatter_a2(i), scatter_b2(i)):
            copy.wait_send()
        for copy in (gather_a(i, x), gather_b(i, y), gather_a2(i, y), gather_b2(i, x)):
            copy.wait_send()

    def sent_z(i):
        for copy in (z_copy(0, i), z_copy(1, i), k_scatter(i), k_gather(i, z)):
            copy.wait_send()

    each(1, SIDE, sent)
    each(1, planes, sent_z)


def solution(mesh):
    replicas, planes = mesh.shape["dp"], mesh.shape["col"]

    def shards(grads, errors, q_init):
        _, rows, cols = grads.shape
        part = rows // replicas
        rank = q_init.shape[1]
        dma = pltpu.SemaphoreType.DMA
        blocks = pltpu.VMEM((SIDE, SIDE, part, cols), BF16)
        line = pltpu.VMEM((SIDE, SIDE, part, cols // 2), BF16)
        single = pltpu.VMEM((SIDE, part, cols // 2), BF16)
        p_f32 = pltpu.VMEM((part, 128), F32)
        chip = 2 * part
        scratch = [
            blocks, blocks, blocks,
            line, line, single, single, single, single,
            blocks,
            pltpu.VMEM((2, part, cols), BF16),
            pltpu.VMEM((2, chip, rows), BF16),
            pltpu.VMEM((planes, chip // 4, rows // 2), BF16),
            pltpu.VMEM((2, planes, part, 128), BF16),
            pltpu.VMEM((2, part, 128), BF16),
            pltpu.VMEM((2, rows, 128), BF16),
            pltpu.VMEM((rows, 128), BF16),
            pltpu.VMEM((128, 256), BF16),
            pltpu.VMEM((2, part, 128), F32), pltpu.VMEM((2, part, 128), F32), p_f32,
            pltpu.VMEM((128, 128), F32), pltpu.VMEM((2, 128, 128), F32),
            pltpu.VMEM((rank, cols), F32), pltpu.VMEM((rank, cols), F32),
            pltpu.VMEM((rank, cols), BF16),
            pltpu.VMEM((rows, rank), BF16),
            dma((replicas,)), dma((replicas,)),
            dma((4, SIDE)), dma((4, SIDE)), dma((4, SIDE)), dma((4, SIDE)),
            dma((2,)),
            dma((2, planes)), dma((2, planes)), dma((planes,)), dma((planes,)), dma((planes,)), dma((planes,)),
            dma((2, replicas)), dma((2, replicas)),
            dma((2, 2)), dma((2, 2)), dma((2,)),
        ]
        vmem = pl.BlockSpec(memory_space=pltpu.VMEM)
        new_errors, q_t = pl.pallas_call(
            functools.partial(kernel, replicas, planes),
            out_shape=(
                jax.ShapeDtypeStruct(grads.shape, BF16),
                jax.ShapeDtypeStruct((rank, cols), F32),
            ),
            in_specs=[pl.BlockSpec(memory_space=pl.ANY)] * 2 + [vmem],
            out_specs=(vmem, vmem),
            scratch_shapes=scratch,
            compiler_params=pltpu.CompilerParams(
                collective_id=0, has_side_effects=True, vmem_limit_bytes=48 * 2**20
            ),
            name="power_round",
        )(grads, errors, q_init.T)
        return new_errors, q_t.T

    return jax.shard_map(
        shards,
        mesh=mesh,
        in_specs=(P("dp", "row", "col"), P("dp", "row", "col"), P("col", None)),
        out_specs=(P("dp", "row", "col"), P("col", None)),
        check_vma=False,
    )
```

time: 229 us -> 165 us (0.72)
  Pallas kernels: 221 us -> 161 us
  local copies, waits for them, and re-layouts: 7.37 us -> 3.31 us
    pallas_call x1, Pallas kernels: 221 us -> 161 us  [shards(): pl.pallas_call(functools.partial(kernel, replicas, planes), out_shape=(ja...]
    unnamed x6 -> x4, local copies, waits for them, and re-layouts: 5.44 us -> 3.31 us
where the time goes in v2:
time: 165 us
  Pallas kernels  161 us (98%)
  local copies, waits for them, and re-layouts  3.31 us (2%)
    pallas_call x1, Pallas kernels, shards(): pl.pallas_call(functools.partial(kernel, replicas, planes), out_shape=(ja...  161 us
    unnamed x4, local copies, waits for them, and re-layouts  3.31 us

profile of v2, /device:TPU:1, one launch (start us, length us, event | category | flops | bytes accessed | tf_op | source)
XLA Modules:
  0.0 165.2 jit_solution(1663919774231855442)
XLA Ops:
  0.6 0.0 copy-start
  0.6 0.9 copy-done
  1.6 161.3 %power_round.1 = (bf16[1,1536,1024]{2,1,0:T(8,128)(2,1)S(1)}, f32[64,1024]{1,0:T(8,128)S(1)}) custom-call(bf16[1,1536,1024]{2,1,0:T(8,128)(2,1)} %g_ref.1, bf16[1,1536,1024]{2,1,0:T(8,128)(2,1)} %e_ref.1, f32[64,1024]{1,0:T(8,128)S(1)} %bitcast.2), custom_call_target="tpu_custom_call" | custom-call | tf_op jit(solution)/shard_map/power_round/pallas_call | solution.py:409
  162.9 1.7 %copy.7 = bf16[1,1536,1024]{2,1,0:T(8,128)(2,1)} copy(bf16[1,1536,1024]{2,1,0:T(8,128)(2,1)S(1)} %get-tuple-element.8) | data formatting | bytes 6291456
  164.5 0.7 copy.8
Async XLA Ops:
  0.6 1.0 copy-start
